TPU v7x, 32 devices: a whole 2x2x4 slice. The times are simulated.
32 devices in a mesh: groups: 2 (over y), tm: 8 (over z, core), chan: 2 (over x), rows: 1.
Axes of the slice: x: 2, y: 2, z: 4, core: 2. Of those that a mesh axis runs over, the one named last changes fastest.
Arguments:
- video: bfloat16 [32, 8, 32, 512], P(('groups', 'tm'), 'rows', None, 'chan'), parts along dimension 0, may hold values from -6 to 6
- channel_gain: float32 [512], P('chan'), may hold values from 0.1 to 1.9
- weights: bfloat16 [27, 512, 512], P(None, None, 'chan'), may hold values from -0.0546875 to 0.0546875
- lengths: int32 [8], P('groups'), parts along dimension 0, may hold values from 1 to 8, 16 in all
- cotangent: bfloat16 [32, 8, 32, 512], P(('groups', 'tm'), 'rows', None, 'chan'), parts along dimension 0, may hold values from -6 to 6
Outputs:
- output: bfloat16 [32, 8, 32, 512], P(('groups', 'tm'), 'rows', None, 'chan'), parts along dimension 0
- input_grad: bfloat16 [32, 8, 32, 512], P(('groups', 'tm'), 'rows', None, 'chan'), parts along dimension 0
- weight_grad: float32 [54, 512, 512], P('groups', ('tm', 'rows'), 'chan'), parts along dimension 0
There are 2 independent parts, one for each index of `groups`. A program takes and returns all parts, laid end to end along the dimension named above; an argument that names none is the same for every part. Nothing has to cross between parts.
Inputs may be any that keep to these rules, and one draw needn't show every extreme that they name: The 4 lengths sum to 16; the longest is exactly 8.
All inputs are finite; a program needn't handle non-finite values.
Results may differ from a plain program's by a relative error of at most 0.004.
Values may be sent and summed in bfloat16 or wider, within the bound.
A program may use at most 128 MiB of HBM per device.

v0:
```python
import math

import jax
import jax.numpy as jnp
from jax import lax
from jax.sharding import PartitionSpec as P


def extended_2(cells, sides, width):
    for axis, dim in sides:
        count = lax.axis_size(axis)
        ends = count - 1
        head = lax.slice_in_dim(cells, 0, width, axis=dim)
        tail = lax.slice_in_dim(cells, cells.shape[dim] - width, cells.shape[dim], axis=dim)
        cells = jnp.concatenate(
            [
                lax.ppermute(tail, axis, [(i, (i + 1) % count) for i in range(ends)]),
                cells,
                lax.ppermute(head, axis, [((i + 1) % count, i) for i in range(ends)]),
            ],
            axis=dim,
        )
    return cells


def shifted(value, axis, steps):
    count = lax.axis_size(axis)
    leading, last = (max(0, -steps), min(count, count - steps))
    return lax.ppermute(value, axis, [(source, source + steps) for source in range(leading, last)])


def clip_tables(lengths, frame_ids):
    clip_ends = jnp.cumsum(lengths)
    clip_starts = clip_ends - lengths
    clip_ids = jnp.sum((frame_ids[:, None] >= clip_ends[None, :]).astype(jnp.int32), axis=1)
    clip_first = jnp.max(
        jnp.where(clip_starts[None, :] <= frame_ids[:, None], clip_starts[None, :], 0), axis=1
    )
    opening = jnp.any(clip_starts[None, :] == frame_ids[:, None], axis=1)
    return (clip_ids, clip_first, opening)


def input_terms(grad_frames, weights, row_count, col_count):
    frame_total = grad_frames.shape[0]
    local_chans = grad_frames.shape[3]
    all_chans = weights.shape[1]
    pieces = []
    for lag_step in range(3):
        back_stack = jnp.stack(
            [
                grad_frames[
                    :,
                    2 - row_step : 2 - row_step + row_count,
                    2 - col_step : 2 - col_step + col_count,
                    :,
                ]
                for row_step in range(3)
                for col_step in range(3)
            ],
            axis=3,
        ).reshape(frame_total * row_count * col_count, 9 * local_chans)
        back_kernel = jnp.transpose(weights[9 * lag_step : 9 * lag_step + 9], (0, 2, 1)).reshape(
            9 * local_chans, all_chans
        )
        pieces.append(
            jnp.dot(back_stack, back_kernel, preferred_element_type=jnp.float32).reshape(
                frame_total, row_count, col_count, all_chans
            )
        )
    return pieces


def lag_mix(lagged, clip_ids, opening, frame_count):
    here_ids = clip_ids[:frame_count]
    start_flag = opening[:frame_count].astype(jnp.float32)
    act_grad = jnp.zeros((frame_count,) + lagged[0].shape[1:], jnp.float32)
    for lag_step in range(3):
        same_clip = (clip_ids[lag_step : lag_step + frame_count] == here_ids).astype(jnp.float32)
        act_grad = (
            act_grad
            + same_clip[:, None, None, None] * lagged[lag_step][lag_step : lag_step + frame_count]
        )
        for inner_step in range(lag_step):
            near_clip = (clip_ids[inner_step : inner_step + frame_count] == here_ids).astype(
                jnp.float32
            ) * start_flag
            act_grad = (
                act_grad
                + near_clip[:, None, None, None]
                * lagged[lag_step][inner_step : inner_step + frame_count]
            )
    return act_grad


def shards(video, channel_gain, weights, lengths, cotangent):
    frame_count, row_count, col_count, local_chans = video.shape
    all_chans = weights.shape[1]
    pixel_count = frame_count * row_count * col_count
    total_pixels = pixel_count * lax.axis_size("tm") * lax.axis_size("rows")
    frame_base = lax.axis_index("tm") * frame_count
    frame_ids = frame_base + jnp.arange(frame_count + 2, dtype=jnp.int32)
    clip_ids, clip_first, opening = clip_tables(lengths, frame_ids)
    own_frames = frame_ids[:frame_count]
    scaled = video.astype(jnp.float32) * channel_gain
    activated = jax.nn.silu(scaled).astype(jnp.bfloat16)
    paired = extended_2(jnp.stack([activated, cotangent]), (("rows", 2),), 1)
    paired = jnp.pad(paired, ((0, 0), (0, 0), (0, 0), (1, 1), (0, 0)))
    act_pad = paired[0]
    grad_pad = paired[1]
    prior_rows = shifted(act_pad, "tm", 1)
    extended = jnp.concatenate([prior_rows, act_pad], axis=0)
    gathered = lax.all_gather(extended, "chan", axis=3, tiled=True)
    flat_grad = cotangent.reshape(pixel_count, local_chans)
    output_sum = jnp.zeros((pixel_count, local_chans), jnp.float32)
    weight_terms = []
    for lag_step in range(3):
        distance = jnp.minimum(lag_step, own_frames - clip_first[:frame_count])[:, None, None, None]
        chosen = jnp.where(
            distance == 0,
            gathered[2 : frame_count + 2],
            jnp.where(distance == 1, gathered[1 : frame_count + 1], gathered[0:frame_count]),
        )
        tap_stack = jnp.stack(
            [
                chosen[:, row_step : row_step + row_count, col_step : col_step + col_count, :]
                for row_step in range(3)
                for col_step in range(3)
            ],
            axis=3,
        ).reshape(pixel_count, 9 * all_chans)
        kernel = weights[9 * lag_step : 9 * lag_step + 9].reshape(9 * all_chans, local_chans)
        output_sum = output_sum + jnp.dot(tap_stack, kernel, preferred_element_type=jnp.float32)
        weight_terms.append(
            lax.dot_general(
                tap_stack, flat_grad, (((0,), (0,)), ((), ())), preferred_element_type=jnp.float32
            ).reshape(9, all_chans, local_chans)
        )
    output = (
        video.astype(jnp.float32)
        + output_sum.reshape(frame_count, row_count, col_count, local_chans)
    ).astype(jnp.bfloat16)
    own_terms = lax.psum_scatter(
        jnp.stack(input_terms(grad_pad, weights, row_count, col_count)),
        "chan",
        scatter_dimension=4,
        tiled=True,
    )
    arriving = shifted(
        jnp.concatenate([own_terms[1, 0:1], own_terms[2, 0:2]], axis=0).astype(jnp.bfloat16),
        "tm",
        -1,
    ).astype(jnp.float32)
    lagged = [
        own_terms[0],
        jnp.concatenate([own_terms[1], arriving[0:1]], axis=0),
        jnp.concatenate([own_terms[2], arriving[1:3]], axis=0),
    ]
    act_grad = lag_mix(lagged, clip_ids, opening, frame_count)
    sigmoid_value = jax.nn.sigmoid(scaled)
    slope_factor = sigmoid_value * (1.0 + scaled * (1.0 - sigmoid_value))
    input_grad = (cotangent.astype(jnp.float32) + act_grad * slope_factor * channel_gain).astype(
        jnp.bfloat16
    )
    weight_sum = jnp.concatenate(weight_terms, axis=0)
    summed = lax.psum_scatter(weight_sum, ("tm", "rows"), scatter_dimension=1, tiled=True)
    weight_grad = summed * (1.0 / math.sqrt(total_pixels))
    return (output, input_grad, weight_grad)


def solution(mesh):
    in_specs = (
        P(("groups", "tm"), "rows", None, "chan"),
        P("chan"),
        P(None, None, "chan"),
        P("groups"),
        P(("groups", "tm"), "rows", None, "chan"),
    )
    out_specs = (
        P(("groups", "tm"), "rows", None, "chan"),
        P(("groups", "tm"), "rows", None, "chan"),
        P("groups", ("tm", "rows"), "chan"),
    )
    return jax.shard_map(shards, mesh=mesh, in_specs=in_specs, out_specs=out_specs, check_vma=False)
```

profile of v0, /device:TPU:0, one launch (start us, length us, event | category | flops | bytes accessed | tf_op | source)
XLA Modules:
  0.0 324.0 jit_solution(5718986588859391785)
XLA Ops:
  10.5 5.9 %fusion.79 = (bf16[9,512,256]{2,1,0:T(8,128)(2,1)S(1)}, bf16[9,512,256]{2,1,0:T(8,128)(2,1)}, bf16[9,512,256]{2,1,0:T(8,128)(2,1)}) fusion(bf16[27,512,256]{2,1,0:T(8,128)(2,1)} %param.7), kind=kLoop, calls=%fused_computation.151 | loop fusion | bytes 14155776 | tf_op jit(solution)/shard_map/slice | solution.py:131
  16.7 2.5 copy.67
  19.2 4.3 %copy.66 = bf16[9,512,256]{1,2,0:T(8,128)(2,1)} copy(bf16[9,512,256]{2,1,0:T(8,128)(2,1)} %get-tuple-element.10) | data formatting | bytes 4718592
  23.5 4.3 %copy.65 = bf16[9,512,256]{1,2,0:T(8,128)(2,1)} copy(bf16[9,512,256]{2,1,0:T(8,128)(2,1)} %get-tuple-element.11) | data formatting | bytes 4718592
  28.8 2.4 collective-permute-start.2
  33.9 3.9 %fusion.13 = f32[1,2,8,32,512]{4,3,2,1,0:T(8,128)S(1)} fusion(bf16[2,8,32,9,256]{4,2,3,1,0:T(8,128)(2,1)} %copy-done.7, bf16[9,512,256]{1,2,0:T(8,128)(2,1)} %copy.67), kind=kOutput, calls=%fused_computation.13 | convolution fusion | flops 1207959552 | bytes 5767168 | tf_op jit(solution)/shard_map/dot_general | solution.py:66
  40.9 2.0 pad_maximum_fusion.1
  43.1 26.7 %all-gather.2.cloned.1.call-done = bf16[4,10,34,512]{3,2,1,0:T(8,128)(2,1)} async-done(((bf16[4,10,34,256]{3,2,1,0:T(8,128)(2,1)}), bf16[4,10,34,512]{3,2,1,0:T(8,128)(2,1)}) %all-gather.2.cloned.1.call-update) | async-done | bytes 1392656 | tf_op jit(solution)/shard_map/all_gather | solution.py:112
  76.1 6.8 %copy.39 = bf16[2,8,32,9,512]{4,3,2,1,0:T(8,128)(2,1)S(1)} copy(bf16[2,8,32,9,512]{4,2,1,0,3:T(8,128)(2,1)} %copy-done.2) | data formatting | bytes 9437184 | tf_op jit(solution)/shard_map/stack | solution.py:123
  83.0 7.6 %copy.68 = bf16[64,8,9,512]{3,1,2,0:T(8,128)(2,1)} copy(bf16[64,8,9,512]{3,2,1,0:T(8,128)(2,1)S(1)} %bitcast.261) | data formatting | bytes 9437184
  97.3 6.5 %copy.42 = bf16[2,8,32,9,512]{4,3,2,1,0:T(8,128)(2,1)S(1)} copy(bf16[2,8,32,9,512]{4,2,1,0,3:T(8,128)(2,1)} %fusion.49) | data formatting | bytes 9437184 | tf_op jit(solution)/shard_map/stack | solution.py:123
  103.8 7.7 %copy.69 = bf16[64,8,9,512]{3,1,2,0:T(8,128)(2,1)} copy(bf16[64,8,9,512]{3,2,1,0:T(8,128)(2,1)S(1)} %bitcast.262) | data formatting | bytes 9437184
  119.8 6.8 %copy.45 = bf16[2,8,32,9,512]{4,3,2,1,0:T(8,128)(2,1)S(1)} copy(bf16[2,8,32,9,512]{4,2,1,0,3:T(8,128)(2,1)} %fusion.40) | data formatting | bytes 9437184 | tf_op jit(solution)/shard_map/stack | solution.py:123
  126.5 7.7 %copy.70 = bf16[64,8,9,512]{3,1,2,0:T(8,128)(2,1)} copy(bf16[64,8,9,512]{3,2,1,0:T(8,128)(2,1)S(1)} %bitcast.263) | data formatting | bytes 9437184
  134.2 6.8 %copy.58 = bf16[4608,512]{1,0:T(8,128)(2,1)} copy(bf16[4608,512]{0,1:T(8,128)(2,1)} %bitcast.277) | data formatting | bytes 9437184 | tf_op jit(solution)/shard_map/dot_general | solution.py:134
  141.0 6.7 %copy.57 = bf16[4608,512]{1,0:T(8,128)(2,1)} copy(bf16[4608,512]{0,1:T(8,128)(2,1)} %bitcast.273) | data formatting | bytes 9437184 | tf_op jit(solution)/shard_map/dot_general | solution.py:134
  147.7 6.7 %copy.56 = bf16[4608,512]{1,0:T(8,128)(2,1)} copy(bf16[4608,512]{0,1:T(8,128)(2,1)} %bitcast.271) | data formatting | bytes 9437184 | tf_op jit(solution)/shard_map/dot_general | solution.py:134
  154.4 3.9 %fusion.83 = f32[9,512,256]{2,1,0:T(8,128)S(1)} fusion(bf16[9,512,512]{2,1,0:T(8,128)(2,1)} %bitcast.270, bf16[512,256,1]{1,0,2:T(8,128)(2,1)S(1)} %bitcast.281), kind=kOutput, calls=%fused_computation.155 | convolution fusion | flops 1207959552 | bytes 9699328 | tf_op jit(solution)/shard_map/dot_general | solution.py:134
  161.1 5.2 %pad_maximum_fusion = f32[27,512,256]{2,1,0:T(8,128)} fusion(f32[9,512,256]{2,1,0:T(8,128)S(1)} %fusion.83, f32[9,512,256]{2,1,0:T(8,128)S(1)} %fusion.82, f32[9,512,256]{2,1,0:T(8,128)S(1)} %fusion.81), kind=kLoop, calls=%fused_computation | loop fusion | flops 7077888 | bytes 28311552 | tf_op jit(solution)/shard_map/concatenate | solution.py:164
  166.7 4.6 %fusion.80 = f32[512,256]{1,0:T(8,128)S(1)} fusion(bf16[512,4608]{1,0:T(8,128)(2,1)} %bitcast.272, bf16[4608,256]{1,0:T(8,128)(2,1)} %bitcast.286), kind=kOutput, calls=%fused_computation.152 | convolution fusion | flops 1207959552 | bytes 7602176 | tf_op jit(solution)/shard_map/dot_general | solution.py:132
  171.5 2.2 convolution_add_fusion.1
  177.3 3.9 %convolution_add_fusion = f32[512,256]{1,0:T(8,128)S(1)} fusion(f32[512,256]{1,0:T(8,128)} %convolution_add_fusion.1, bf16[512,4608]{1,0:T(8,128)(2,1)} %bitcast.278, bf16[4608,256]{1,0:T(8,128)(2,1)S(1)} %bitcast.284), kind=kOutput, calls=%fused_computation.14 | convolution fusion | flops 1208090624 | bytes 8126464 | tf_op jit(solution)/shard_map/dot_general | solution.py:132
  182.7 131.7 %reduce-scatter.5.cloned.1.call-done = f32[27,64,256]{2,1,0:T(8,128)} async-done(((f32[27,512,256]{2,1,0:T(8,128)}), f32[27,64,256]{2,1,0:T(8,128)}) %reduce-scatter.5.cloned.1.call-update) | async-done | bytes 1769488 | tf_op jit(solution)/shard_map/reduce_scatter | solution.py:165
  314.4 2.9 broadcast_multiply_fusion
  (112 shorter events, 40.0 us)
Async XLA Ops:
  7.2 62.7 %all-gather.2.cloned.1.call-start = ((), (), s32[]{:S(2)}) async-start(), calls=%async_computation.2 | async-start | bytes 2457600 | tf_op jit(solution)/shard_map/all_gather | solution.py:112
  9.1 18.7 %collective-permute-start.1 = (bf16[2,2,1,32,256]{4,3,2,1,0:T(8,128)(2,1)S(1)}, bf16[2,2,1,32,256]{4,3,2,1,0:T(8,128)(2,1)S(1)}, u32[]{:S(2)}, u32[]{:S(2)}) collective-permute-start(bf16[2,2,1,32,256]{4,3,2,1,0:T(8,128)(2,1)S(1)} %get-tuple-element.20), channel_id=1, source_target_pairs={} | collective-permute-start | bytes 196616 | tf_op jit(solution)/shard_map/ppermute | solution.py:19
  9.8 18.0 %collective-permute-start = (bf16[2,2,1,32,256]{4,3,2,1,0:T(8,128)(2,1)S(1)}, bf16[2,2,1,32,256]{4,3,2,1,0:T(8,128)(2,1)S(1)}, u32[]{:S(2)}, u32[]{:S(2)}) collective-permute-start(bf16[2,2,1,32,256]{4,3,2,1,0:T(8,128)(2,1)S(1)} %get-tuple-element.19), channel_id=1, source_target_pairs={} | collective-permute-start | bytes 196616 | tf_op jit(solution)/shard_map/ppermute | solution.py:17
  10.5 5.9 %copy-start.10 = (s32[4]{0:T(128)S(1)}, s32[4]{0:T(128)}, u32[]{:S(2)}) copy-start(s32[4]{0:T(128)} %param.8) | copy-start | bytes 52
  19.2 8.6 %copy-start = (bf16[2,8,32,256]{3,2,1,0:T(8,128)(2,1)S(1)}, bf16[2,8,32,256]{3,2,1,0:T(8,128)(2,1)}, u32[]{:S(2)}) copy-start(bf16[2,8,32,256]{3,2,1,0:T(8,128)(2,1)} %param.9) | copy-start | bytes 786436
  28.8 3.7 %collective-permute-start.2 = (bf16[2,10,34,256]{3,2,1,0:T(8,128)(2,1)S(1)}, bf16[2,10,34,256]{3,2,1,0:T(8,128)(2,1)S(1)}, u32[]{:S(2)}, u32[]{:S(2)}) collective-permute-start(bf16[2,10,34,256]{3,2,1,0:T(8,128)(2,1)S(1)} %get-tuple-element.18), channel_id=1, source_target_pairs={{0,2},{2,4},{4,6},{6,8},{8,10},{10,12},{12,14},{1,3},{3,5},{5,7},{... | collective-permute-start | bytes 1044488 | tf_op jit(solution)/shard_map/ppermute | solution.py:29
  31.3 1.5 copy-start.7
  33.8 139.8 %reduce-scatter.3.cloned.1.call-start = ((), (), s32[]{:S(2)}) async-start(), calls=%async_computation.3 | async-start | bytes 4718592 | tf_op jit(solution)/shard_map/reduce_scatter | solution.py:142
  33.9 3.9 %copy-start.4 = (bf16[9,512,256]{1,2,0:T(8,128)(2,1)S(1)}, bf16[9,512,256]{1,2,0:T(8,128)(2,1)}, u32[]{:S(2)}) copy-start(bf16[9,512,256]{1,2,0:T(8,128)(2,1)} %copy.66) | copy-start | bytes 7077892
  33.9 3.9 %copy-start.8 = (bf16[2,8,32,9,256]{4,2,3,1,0:T(8,128)(2,1)S(1)}, bf16[2,8,32,9,256]{4,2,3,1,0:T(8,128)(2,1)}, u32[]{:S(2)}) copy-start(bf16[2,8,32,9,256]{4,2,3,1,0:T(8,128)(2,1)} %copy-done.7) | copy-start | bytes 7077892
  37.8 1.7 copy-start.5
  42.9 271.5 %reduce-scatter.5.cloned.1.call-start = ((), (), s32[]{:S(2)}) async-start(), calls=%async_computation.4 | async-start | bytes 15925248 | tf_op jit(solution)/shard_map/reduce_scatter | solution.py:165
  72.9 2.3 copy-start.2
  147.7 10.6 %slice-start.2 = ((s8[4718592]{0:T(1024)(128)(4,1)}), s8[524288]{0:T(1024)(128)(4,1)S(1)}, s32[]{:S(2)}) async-start(s8[4718592]{0:T(1024)(128)(4,1)} %bitcast.267), calls=%async_computation.7 | async-start | bytes 1048576
  154.4 3.9 %slice-start.3 = ((s8[4718592]{0:T(1024)(128)(4,1)}), s8[4194304]{0:T(1024)(128)(4,1)S(1)}, s32[]{:S(2)}) async-start(s8[4718592]{0:T(1024)(128)(4,1)} %bitcast.267), calls=%async_computation.8 | async-start | bytes 8388608
  154.4 5.3 %slice-start = ((s8[4718592]{0:T(1024)(128)(4,1)}), s8[4194304]{0:T(1024)(128)(4,1)S(1)}, s32[]{:S(2)}) async-start(s8[4718592]{0:T(1024)(128)(4,1)} %bitcast.264), calls=%async_computation.5 | async-start | bytes 8388608
  158.3 1.4 slice-start.1
  166.4 5.0 %slice-start.4 = ((s8[4718592]{0:T(1024)(128)(4,1)}), s8[4194304]{0:T(1024)(128)(4,1)S(1)}, s32[]{:S(2)}) async-start(s8[4718592]{0:T(1024)(128)(4,1)} %bitcast.274), calls=%async_computation.9 | async-start | bytes 8388608
  166.4 5.0 %copy-start.1 = (bf16[9,512,256]{2,1,0:T(8,128)(2,1)S(1)}, bf16[9,512,256]{2,1,0:T(8,128)(2,1)}, u32[]{:S(2)}) copy-start(bf16[9,512,256]{2,1,0:T(8,128)(2,1)} %get-tuple-element.10) | copy-start | bytes 7077892
  166.7 4.8 %slice-start.5 = ((s8[4718592]{0:T(1024)(128)(4,1)}), s8[524288]{0:T(1024)(128)(4,1)S(1)}, s32[]{:S(2)}) async-start(s8[4718592]{0:T(1024)(128)(4,1)} %bitcast.274), calls=%async_computation.10 | async-start | bytes 1048576
  175.7 5.4 %copy-start.3 = (f32[3,2,8,32,256]{4,3,2,1,0:T(8,128)S(1)}, f32[3,2,8,32,256]{4,3,2,1,0:T(8,128)}, u32[]{:S(2)}) copy-start(f32[3,2,8,32,256]{4,3,2,1,0:T(8,128)} %reduce-scatter.3.cloned.1.call-done) | copy-start | bytes 4718596
  175.8 5.5 %collective-permute-start.3 = (bf16[3,8,32,256]{3,2,1,0:T(8,128)(2,1)S(1)}, bf16[3,8,32,256]{3,2,1,0:T(8,128)(2,1)S(1)}, u32[]{:S(2)}, u32[]{:S(2)}) collective-permute-start(bf16[3,8,32,256]{3,2,1,0:T(8,128)(2,1)S(1)} %pad_maximum_fusion.5), channel_id=1, source_target_pairs={{2,0},{4,2},{6,4},{8,6},{10,8},{12,10},{14,12},{3,1},{5,3},{7,5},{... | collective-permute-start | bytes 1179656 | tf_op jit(solution)/shard_map/ppermute | solution.py:29
  177.2 4.1 %copy-start.6 = (bf16[2,8,32,256]{3,2,1,0:T(8,128)(2,1)S(1)}, bf16[2,8,32,256]{3,2,1,0:T(8,128)(2,1)}, u32[]{:S(2)}) copy-start(bf16[2,8,32,256]{3,2,1,0:T(8,128)(2,1)} %param.5) | copy-start | bytes 786436
  177.2 4.1 %copy-start.9 = (f32[256]{0:T(256)S(1)}, f32[256]{0:T(256)}, u32[]{:S(2)}) copy-start(f32[256]{0:T(256)} %param.6) | copy-start | bytes 3076
Sparse Core Ops, SparseCore 0:
  34.0 35.8 all-gather.1
  72.1 43.3 reduce-scatter.2
  166.5 147.8 reduce-scatter.4
where the time goes:
time: 329 us; the launch traced here: 324 us
  waiting for transfers between devices  160 us (49%)
  local copies, waits for them, and re-layouts  103 us (31%)
  matrix products  24 us (7%)
  other arithmetic  17.4 us (5%)
  between operations  14.5 us (4%)
  starting transfers between devices  5.41 us (2%)
    reduce_scatter x1, waiting for transfers between devices, shards(): lax.psum_scatter(weight_sum, ('tm', 'rows'), scatter_dimension=1, tiled=T...  132 us
    unnamed x72, local copies, waits for them, and re-layouts  52.4 us
    all_gather x1, waiting for transfers between devices, shards(): gathered = lax.all_gather(extended, 'chan', axis=3, tiled=True)  26.7 us
    another operation x6, local copies, waits for them, and re-layouts, shards(): jnp.stack([chosen[:, row_step:row_step + row_count, col_step:col_step + c...  22.3 us
    dot_general x3, local copies, waits for them, and re-layouts, shards(): lax.dot_general(tap_stack, flat_grad, (((0,), (0,)), ((), ())), preferred...  20.2 us
    dot_general x3, matrix products, shards(): jnp.dot(tap_stack, kernel, preferred_element_type=jnp.float32)  10.7 us
    dot_general x3, matrix products, input_terms(): jnp.dot(back_stack, back_kernel, preferred_element_type=jnp.float32)  6.66 us
    dot_general x3, matrix products, shards(): lax.dot_general(tap_stack, flat_grad, (((0,), (0,)), ((), ())), preferred...  6.65 us
  transfers between devices with their start and end apart: 7, of which 3 were waited for; matrix products, arithmetic and copies ran while one was open for 42% of the time, Pallas kernels for 0%

commit v1 on v0

v1 whole, which is shorter than its diff:
```python
import functools
import math

import jax
import jax.numpy as jnp
from jax import lax
from jax.experimental import pallas as pl
from jax.experimental.pallas import tpu as pltpu
from jax.sharding import PartitionSpec as P

MESH = pl.DeviceIdType.MESH
LAGS = 3
SIDE = 3
TAPS = SIDE * SIDE


def clip_tables(lengths, frame_ids):
    order = jnp.arange(lengths.shape[0], dtype=jnp.int32)
    clip_ends = jnp.sum(
        jnp.where(order[None, :] <= order[:, None], lengths[None, :], 0), axis=1
    ).astype(jnp.int32)
    clip_starts = clip_ends - lengths
    clip_ids = jnp.sum((frame_ids[:, None] >= clip_ends[None, :]).astype(jnp.int32), axis=1)
    clip_first = jnp.max(
        jnp.where(clip_starts[None, :] <= frame_ids[:, None], clip_starts[None, :], 0), axis=1
    )
    opening = jnp.any(clip_starts[None, :] == frame_ids[:, None], axis=1)
    return (clip_ids, clip_first, opening)


def kernel(
    dims,
    table_ref,
    coef_ref,
    act_ref,
    act_t_ref,
    cot_ref,
    w_ref,
    out_ref,
    grad_ref,
    wgrad_ref,
    x_prev,
    x_own,
    cots,
    act_ts,
    w_buf,
    pad_x,
    pad_g,
    stack,
    partial,
    p_out,
    p_in,
    w_sem,
    xp_send,
    xp_recv,
    xo_send,
    xo_recv,
    cot_send,
    cot_recv,
    at_send,
    at_recv,
    p_send,
    p_recv,
):
    n_tm, n_chan, n_rows, frames, height, width, own = dims
    t, c = lax.axis_index("tm"), lax.axis_index("chan")
    r = lax.axis_index("rows") if n_rows > 1 else 0
    pixels = n_rows * height * width
    local = height * width
    block = act_ts.shape[1]
    pair = 2 if n_tm % 2 == 0 else 1
    side, place, places = t % pair, t // pair, n_tm // pair
    sibling = t + 1 - 2 * side

    load_w = pltpu.make_async_copy(w_ref, w_buf, w_sem)
    load_w.start()

    barrier = pltpu.get_barrier_semaphore()
    for tt in range(n_tm):
        for cc in range(n_chan):

            @pl.when((tt != t) | (cc != c))
            def _():
                pl.semaphore_signal(
                    barrier, inc=1, device_id={"tm": tt, "chan": cc}, device_id_type=MESH
                )

    x_own[c] = act_ref[...]
    cots[t] = cot_ref[...]
    pl.semaphore_wait(barrier, n_tm * n_chan - 1)

    def send_own(cc):
        return pltpu.make_async_remote_copy(
            act_ref, x_own.at[c], xo_send.at[cc], xo_recv.at[c],
            device_id={"chan": cc}, device_id_type=MESH,
        )

    def send_prev(cc):
        return pltpu.make_async_remote_copy(
            act_ref.at[pl.ds((frames - 2) * pixels, 2 * pixels)], x_prev.at[c],
            xp_send.at[cc], xp_recv.at[c],
            device_id={"tm": t + 1, "chan": cc}, device_id_type=MESH,
        )

    def send_cot(s, way, to):
        return pltpu.make_async_remote_copy(
            cots.at[s], cots.at[s], cot_send.at[way, s], cot_recv.at[s],
            device_id={"tm": to}, device_id_type=MESH,
        )

    def send_at(tt, cc):
        row = (tt * n_rows + r) * block - c * own
        if n_rows > 1:
            row = pl.multiple_of(row, 16)
        return pltpu.make_async_remote_copy(
            act_t_ref.at[pl.ds(row, block)], act_ts.at[t], at_send.at[tt, cc], at_recv.at[t],
            device_id={"tm": tt, "chan": cc}, device_id_type=MESH,
        )

    def for_at(act):
        for step in range(n_tm):
            for cc in range(n_chan):
                tt = step
                mine = ((tt * n_rows + r) * block) // own == c

                @pl.when(mine & ((tt != t) | (cc != c)))
                def _():
                    act(tt, cc)

    def arrived(ref, sem):
        pltpu.make_async_remote_copy(
            ref, ref, sem, sem, device_id={"tm": t}, device_id_type=MESH
        ).wait_recv()

    def cot_moves(s, from_left, act):
        if from_left is not False:

            @pl.when(place + 1 < places)
            def _():
                act(s, 0, t + pair)

        if from_left is not True:

            @pl.when(place > 0)
            def _():
                act(s, 1, t - pair)

        if pair == 2:
            act(s, 2, sibling)

    def start_cot(s, way, to):
        send_cot(s, way, to).start()

    def finish_cot(s, way, to):
        send_cot(s, way, to).wait_send()

    def hop(d):
        @pl.when(place - d >= 0)
        def _():
            s = t - pair * d
            arrived(cots.at[s], cot_recv.at[s])
            cot_moves(s, True, start_cot)

        @pl.when(place + d < places)
        def _():
            s = t + pair * d
            arrived(cots.at[s], cot_recv.at[s])
            cot_moves(s, False, start_cot)

    cot_moves(t, None, start_cot)
    for cc in range(n_chan):

        @pl.when(cc != c)
        def _():
            send_own(cc).start()

        @pl.when(t + 1 < n_tm)
        def _():
            send_prev(cc).start()

    for_at(lambda tt, cc: send_at(tt, cc).start())
    row0 = (t * n_rows + r) * block

    @pl.when(row0 // own == c)
    def _():
        act_ts[t] = act_t_ref[pl.ds(pl.multiple_of(row0 - c * own, 16), block), :]

    column = lax.broadcasted_iota(jnp.int32, (pixels, 1), 0) % width

    def columns(value, step):
        if step == 0:
            return value
        moved = pltpu.roll(value, (-step) % pixels, axis=0)
        return jnp.where((column + step >= 0) & (column + step < width), moved, 0.0)

    edge = (n_rows * height + 1) * width

    def fill(ref, value, sign):
        for b in range(SIDE):
            ref[b, pl.ds(width, pixels), :] = columns(value, sign * (b - 1)).astype(jnp.bfloat16)

    pad_x[:, :, :width, :] = jnp.zeros_like(pad_x[:, :, :width, :])
    pad_x[:, :, edge:, :] = jnp.zeros_like(pad_x[:, :, edge:, :])
    pad_g[:, :, :, :width, :] = jnp.zeros_like(pad_g[:, :, :, :width, :])
    pad_g[:, :, :, edge:, :] = jnp.zeros_like(pad_g[:, :, :, edge:, :])
    partial[...] = jnp.zeros_like(partial)
    out_ref[...] = jnp.zeros_like(out_ref)
    wgrad_ref[...] = jnp.zeros_like(wgrad_ref)

    if places > 1:
        hop(1)

    if pair == 2:

        @pl.when(side == 0)
        def _():
            arrived(cots.at[sibling], cot_recv.at[sibling])

        @pl.when((side == 1) & (t + 1 < n_tm))
        def _():
            arrived(cots.at[t + 1], cot_recv.at[t + 1])

    def cot_frame(f):
        frame = jnp.minimum(t * frames + f, n_tm * frames - 1)
        return cots[frame // frames, pl.ds((frame % frames) * pixels, pixels), :].astype(jnp.float32)

    for f in range(frames):
        near = [cot_frame(f + m) for m in range(LAGS)]
        for lag in range(LAGS):
            mixed = sum(coef_ref[(f * LAGS + lag) * LAGS + m] * near[m] for m in range(lag + 1))
            fill(pad_g.at[f, lag], mixed, -1)

    load_w.wait()

    def back(k, _):
        lag, a, b = k // TAPS, (k % TAPS) // SIDE, k % SIDE
        start = pl.multiple_of((r * height + 2 - a) * width, 16)
        grads = jnp.concatenate(
            [pad_g[f, lag, b, pl.ds(start, local), :] for f in range(frames)], axis=0
        )
        partial[...] += lax.dot_general(
            grads, w_buf[k], (((1,), (1,)), ((), ())), preferred_element_type=jnp.float32
        )
        return 0

    lax.fori_loop(0, LAGS * TAPS, back, 0)

    def send_p(cc):
        return pltpu.make_async_remote_copy(
            p_out.at[cc], p_in.at[c], p_send.at[cc], p_recv.at[c],
            device_id={"chan": cc}, device_id_type=MESH,
        )

    for cc in range(n_chan):

        @pl.when(cc != c)
        def _():
            p_out[cc] = partial[:, cc * own : (cc + 1) * own].astype(jnp.bfloat16)
            send_p(cc).start()

    if places > 2:
        hop(2)

    for cc in range(n_chan):

        @pl.when(cc != c)
        def _():
            arrived(x_own.at[cc], xo_recv.at[cc])

        @pl.when(t > 0)
        def _():
            arrived(x_prev.at[cc], xp_recv.at[cc])

    for cc in range(n_chan):
        for slot in range(2 + frames):
            if slot < 2:
                value = x_prev[cc, slot * pixels : (slot + 1) * pixels, :]
            else:
                value = x_own[cc, (slot - 2) * pixels : (slot - 1) * pixels, :]
            fill(
                pad_x.at[slot, :, :, cc * own : (cc + 1) * own], value.astype(jnp.float32), 1
            )

    if places > 3:
        hop(3)

    def ahead(k, _):
        lag, a, b = k // TAPS, (k % TAPS) // SIDE, k % SIDE
        start = pl.multiple_of((r * height + a) * width, 16)
        taps = jnp.concatenate(
            [
                pad_x[table_ref[f * LAGS + lag], b, pl.ds(start, local), :]
                for f in range(frames)
            ],
            axis=0,
        )
        out_ref[...] += jnp.dot(taps, w_buf[k], preferred_element_type=jnp.float32)
        return 0

    lax.fori_loop(0, LAGS * TAPS, ahead, 0)

    for d in range(4, places):
        hop(d)

    place_of = lax.broadcasted_iota(jnp.int32, (1, pixels), 1)
    line, spot = place_of // width, place_of % width

    for_owner = row0 // own != c

    def build(s, _):
        @pl.when((s != t) | for_owner)
        def _():
            arrived(act_ts.at[s], at_recv.at[s])

        for f in range(frames):
            value = act_ts[s, :, f * pixels : (f + 1) * pixels].astype(jnp.float32)
            for k in range(TAPS):
                down, right = k // SIDE - 1, k % SIDE - 1
                step = down * width + right
                moved = value if step == 0 else pltpu.roll(value, (-step) % pixels, axis=1)
                inside = (
                    (line + down >= 0)
                    & (line + down < n_rows * height)
                    & (spot + right >= 0)
                    & (spot + right < width)
                )
                stack[s * frames + f, k * block : (k + 1) * block, :] = jnp.where(
                    inside, moved, 0.0
                ).astype(jnp.bfloat16)
        return 0

    lax.fori_loop(0, n_tm, build, 0)

    if pair == 2:
        for q in range(places):
            s = q * pair + 1 - side
            early = ((side == 0) & (s == sibling)) | ((side == 1) & (s == t + 1))

            @pl.when(jnp.logical_not(early))
            def _():
                arrived(cots.at[s], cot_recv.at[s])

    def weigh(s, _):
        for lag in range(LAGS):
            taps = jnp.concatenate(
                [
                    stack[table_ref[frames * LAGS + (s * frames + f) * LAGS + lag]]
                    for f in range(frames)
                ],
                axis=1,
            )
            rows = pl.ds(lag * TAPS * block, TAPS * block)
            wgrad_ref[rows, :] += jnp.dot(taps, cots[s], preferred_element_type=jnp.float32)
        return 0

    lax.fori_loop(0, n_tm, weigh, 0)

    total = partial[:, pl.ds(pl.multiple_of(c * own, 128), own)]
    grad_ref[...] = total
    for cc in range(n_chan):

        @pl.when(cc != c)
        def _():
            arrived(p_in.at[cc], p_recv.at[cc])
            grad_ref[...] += p_in[cc].astype(jnp.float32)
            send_p(cc).wait_send()
            send_own(cc).wait_send()

        @pl.when(t + 1 < n_tm)
        def _():
            send_prev(cc).wait_send()

    for_at(lambda tt, cc: send_at(tt, cc).wait_send())
    cot_moves(t, None, finish_cot)
    for d in range(1, places):

        @pl.when(place - d >= 0)
        def _():
            cot_moves(t - pair * d, True, finish_cot)

        @pl.when(place + d < places)
        def _():
            cot_moves(t + pair * d, False, finish_cot)


def shards(video, channel_gain, weights, lengths, cotangent):
    frame_count, row_count, col_count, own = video.shape
    taps, all_chans, _ = weights.shape
    n_tm, n_chan, n_rows = (lax.axis_size(a) for a in ("tm", "chan", "rows"))
    local_count = frame_count * row_count * col_count
    total_pixels = local_count * n_tm * n_rows
    all_frames = n_tm * frame_count
    block = all_chans // (n_tm * n_rows)
    frame_base = lax.axis_index("tm") * frame_count
    frame_ids = jnp.arange(all_frames + 2, dtype=jnp.int32)
    clip_ids, clip_first, opening = clip_tables(lengths, frame_ids)
    lags = jnp.arange(LAGS, dtype=jnp.int32)
    sources = jnp.maximum(frame_ids[:all_frames, None] - lags, clip_first[:all_frames, None])
    mine = lax.dynamic_slice_in_dim(sources, frame_base, frame_count, 0)
    table = jnp.concatenate([(mine - frame_base + 2).reshape(-1), sources.reshape(-1)])
    ids = lax.dynamic_slice_in_dim(clip_ids, frame_base, frame_count + 2, 0)
    opens = lax.dynamic_slice_in_dim(opening, frame_base, frame_count, 0)
    same = jnp.stack([ids[m : m + frame_count] == ids[:frame_count] for m in range(LAGS)], axis=1)
    coef = jnp.where(
        lags[None, :, None] == lags[None, None, :],
        same[:, None, :],
        (lags[None, None, :] < lags[None, :, None]) & same[:, None, :] & opens[:, None, None],
    ).astype(jnp.float32).reshape(-1)

    scaled = video.astype(jnp.float32) * channel_gain
    activated = jax.nn.silu(scaled).astype(jnp.bfloat16)
    act_full, cot_full = activated, cotangent
    if n_rows > 1:
        act_full = lax.all_gather(activated, "rows", axis=1, tiled=True)
        cot_full = lax.all_gather(cotangent, "rows", axis=1, tiled=True)
    act_full = act_full.reshape(-1, own)
    cot_full = cot_full.reshape(-1, own)
    act_t = act_full.T

    full = act_full.shape[0]
    pixels = full // frame_count
    padded = pixels + 2 * col_count
    vmem = pl.BlockSpec(memory_space=pltpu.VMEM)
    smem = pl.BlockSpec(memory_space=pltpu.SMEM)
    bf16, f32 = jnp.bfloat16, jnp.float32
    dma = pltpu.SemaphoreType.DMA
    out_sum, act_grad, weight_sum = pl.pallas_call(
        functools.partial(
            kernel, (n_tm, n_chan, n_rows, frame_count, row_count, col_count, own)
        ),
        out_shape=(
            jax.ShapeDtypeStruct((local_count, own), f32),
            jax.ShapeDtypeStruct((local_count, own), f32),
            jax.ShapeDtypeStruct((taps * block, own), f32),
        ),
        in_specs=[smem, smem, vmem, vmem, vmem, pl.BlockSpec(memory_space=pl.ANY)],
        out_specs=(vmem, vmem, vmem),
        scratch_shapes=[
            pltpu.VMEM((n_chan, 2 * pixels, own), bf16),
            pltpu.VMEM((n_chan, full, own), bf16),
            pltpu.VMEM((n_tm, full, own), bf16),
            pltpu.VMEM((n_tm, block, full), bf16),
            pltpu.VMEM(weights.shape, bf16),
            pltpu.VMEM((2 + frame_count, SIDE, padded, all_chans), bf16),
            pltpu.VMEM((frame_count, LAGS, SIDE, padded, own), bf16),
            pltpu.VMEM((all_frames, TAPS * block, pixels), bf16),
            pltpu.VMEM((local_count, all_chans), f32),
            pltpu.VMEM((n_chan, local_count, own), bf16),
            pltpu.VMEM((n_chan, local_count, own), bf16),
            dma,
            dma((n_chan,)),
            dma((n_chan,)),
            dma((n_chan,)),
            dma((n_chan,)),
            dma((3, n_tm)),
            dma((n_tm,)),
            dma((n_tm, n_chan)),
            dma((n_tm,)),
            dma((n_chan,)),
            dma((n_chan,)),
        ],
        compiler_params=pltpu.CompilerParams(
            collective_id=0, has_side_effects=True, vmem_limit_bytes=56 * 2**20
        ),
        cost_estimate=pl.CostEstimate(
            flops=6 * local_count * taps * all_chans * own,
            bytes_accessed=2 * weights.size + 4 * taps * block * own,
            transcendentals=0,
        ),
    )(table, coef, act_full, act_t, cot_full, weights)

    output = (video.astype(f32) + out_sum.reshape(video.shape)).astype(bf16)
    sigmoid_value = jax.nn.sigmoid(scaled)
    slope_factor = sigmoid_value * (1.0 + scaled * (1.0 - sigmoid_value))
    input_grad = (
        cotangent.astype(f32) + act_grad.reshape(video.shape) * slope_factor * channel_gain
    ).astype(bf16)
    weight_grad = weight_sum.reshape(taps, block, own) * (1.0 / math.sqrt(total_pixels))
    return (output, input_grad, weight_grad)


def solution(mesh):
    in_specs = (
        P(("groups", "tm"), "rows", None, "chan"),
        P("chan"),
        P(None, None, "chan"),
        P("groups"),
        P(("groups", "tm"), "rows", None, "chan"),
    )
    out_specs = (
        P(("groups", "tm"), "rows", None, "chan"),
        P(("groups", "tm"), "rows", None, "chan"),
        P("groups", ("tm", "rows"), "chan"),
    )
    return jax.shard_map(shards, mesh=mesh, in_specs=in_specs, out_specs=out_specs, check_vma=False)
```

time: 329 us -> 77.2 us (0.23); the launches traced: 324 us -> 76.7 us
  waiting for transfers between devices: 160 us -> 0 us
  local copies, waits for them, and re-layouts: 103 us -> 1.75 us
  Pallas kernels: 0 us -> 66.4 us
  matrix products: 24 us -> 0 us
  between operations: 14.5 us -> 0.73 us
  other arithmetic: 17.4 us -> 7.9 us
  starting transfers between devices: 5.41 us -> 0 us
    reduce_scatter x2 -> x0, waiting for transfers between devices: 132 us -> none  [the longest x1 132 us: shards(): lax.psum_scatter(weight_sum, ('tm', 'rows'), scatter_dimension=1, tiled=T...]
    pallas_call x0 -> x1, Pallas kernels: none -> 66.4 us  [shards(): pl.pallas_call(functools.partial(kernel, (n_tm, n_chan, n_rows, frame_cou...]
    unnamed x72 -> x10, local copies, waits for them, and re-layouts: 52.4 us -> 0.02 us
    all_gather x1 -> x0, waiting for transfers between devices: 26.7 us -> none  [shards(): gathered = lax.all_gather(extended, 'chan', axis=3, tiled=True)]
    dot_general x9 -> x0, matrix products: 24 us -> none  [the longest x3 10.7 us: shards(): jnp.dot(tap_stack, kernel, preferred_element_type=jnp.float32)]
    another operation x8 -> x2, local copies, waits for them, and re-layouts: 23.4 us -> 0.12 us  [shards(): jnp.stack([ids[m:m + frame_count] == ids[:frame_count] for m in range(LAG...]
    dot_general x3 -> x0, local copies, waits for them, and re-layouts: 20.2 us -> none  [shards(): lax.dot_general(tap_stack, flat_grad, (((0,), (0,)), ((), ())), preferred...]
    concatenate x4 -> x1, other arithmetic: 6.66 us -> 0.59 us  [shards(): jnp.concatenate([(mine - frame_base + 2).reshape(-1), sources.reshape(-1)])]
  transfers between devices with their start and end apart: 7 -> 0, of which waited for: 3 -> 0; matrix products, arithmetic and copies ran while one was open for 42% -> 0% of each run, Pallas kernels for 0% -> 0%
where the time goes in v1:
time: 77.2 us; the launch traced here: 76.7 us
  Pallas kernels  66.4 us (86%)
  other arithmetic  7.9 us (10%)
  local copies, waits for them, and re-layouts  1.75 us (2%)
    pallas_call x1, Pallas kernels, shards(): pl.pallas_call(functools.partial(kernel, (n_tm, n_chan, n_rows, frame_cou...  66.4 us
    convert_element_type x1, other arithmetic, shards(): input_grad = (cotangent.astype(f32) + act_grad.reshape(video.shape) * slo...  2.39 us

profile of v1, /device:TPU:0, one launch (start us, length us, event | category | flops | bytes accessed | tf_op | source)
XLA Modules:
  0.0 76.7 jit_solution(17634838419248739457)
XLA Ops:
  0.6 0.8 %select_reduce_fusion.1 = s32[4]{0:T(128)S(1)} fusion(s32[4]{0:T(128)} %param.8), kind=kLoop, calls=%fused_computation.25 | loop fusion | flops 44 | bytes 32 | tf_op jit(solution)/shard_map/reduce_sum | solution.py:19
  1.4 0.7 sub.30
  2.1 0.1 convert_reduce_fusion
  2.2 0.1 dynamic_slice.10
  2.2 0.1 select_reduce_fusion
  2.3 0.1 fusion.14
  2.4 0.1 dynamic_slice.11
  2.5 0.1 and.29
  2.6 0.1 and.30
  2.7 0.1 broadcast_in_dim.40
  2.8 0.1 and.27
  2.9 0.1 compare_bitcast_fusion.1
  2.9 0.1 pad_add_fusion
  3.0 0.1 copy.13
  3.1 0.1 broadcast_in_dim.48
  3.2 0.6 select_convert_fusion.coef_ref
  3.9 0.1 max.14
  4.0 0.1 reshape.74
  4.0 0.6 pad_add_fusion.1.table_ref
  4.6 1.1 %fusion.6 = bf16[2,8,32,256]{3,2,1,0:T(8,128)(2,1)S(1)} fusion(bf16[2,8,32,256]{3,2,1,0:T(8,128)(2,1)} %param.5, f32[256]{0:T(256)} %param.6), kind=kLoop, calls=%fused_computation.9 | loop fusion | flops 917504 | bytes 525312 | tf_op jit(solution)/shard_map/convert_element_type | solution.py:411
  5.8 0.8 %copy.14 = bf16[512,256]{0,1:T(8,128)(2,1)} copy(bf16[512,256]{1,0:T(8,128)(2,1)S(1)} %bitcast.14) | data formatting | bytes 524288 | tf_op jit(solution)/shard_map/reshape | solution.py:416
  6.6 66.4 %shard_map.76 = (f32[512,256]{1,0:T(8,128)}, f32[512,256]{1,0:T(8,128)}, f32[1728,256]{1,0:T(8,128)}) custom-call(s32[54]{0:T(128)} %pad_add_fusion.1.table_ref, f32[18]{0:T(128)} %select_convert_fusion.coef_ref, bf16[512,256]{1,0:T(8,128)(2,1)} %bitcast.15, bf16[256,512]{1,0:T(8,128)(2,1)} %bitcast.18, bf16[512,256]{1,0:T(8,128)(2,1)} %bitcast.19, ...), custom_call_target="tpu_custom_call" | custom-call | flops 10871635968 | bytes 8847360 | tf_op jit(solution)/shard_map/pallas_call | solution.py:427
  73.0 2.4 %fusion.12 = (bf16[2,8,32,256]{3,2,1,0:T(8,128)(2,1)}, bf16[2,8,32,256]{3,2,1,0:T(8,128)(2,1)}) fusion(f32[2,8,32,256]{3,2,1,0:T(8,128)} %bitcast.17, bf16[2,8,32,256]{3,2,1,0:T(8,128)(2,1)S(1)} %copy-done.2, bf16[2,8,32,256]{3,2,1,0:T(8,128)(2,1)S(1)} %copy-done.3, f32[256]{0:T(256)S(1)} %copy-done.4, f32[2,8,32,256]{3,2,1,0:T(8,128)} %bitcast.16), kind=kLoop, calls=%fused_computation.15 | loop fusion | flops 2097152 | bytes 2098176 | tf_op jit(solution)/shard_map/convert_element_type | solution.py:477
  75.4 1.3 %broadcast_multiply_fusion = f32[1728,256]{1,0:T(8,128)} fusion(f32[1728,256]{1,0:T(8,128)S(1)} %copy-done), kind=kLoop, calls=%fused_computation | loop fusion | flops 442368 | bytes 3538944 | tf_op jit(solution)/shard_map/mul | solution.py:478
  (19 shorter events, 0.1 us)
Async XLA Ops:
  5.7 0.9 %copy-start.1 = (bf16[2,8,32,256]{3,2,1,0:T(8,128)(2,1)}, bf16[2,8,32,256]{3,2,1,0:T(8,128)(2,1)S(1)}, u32[]{:S(2)}) copy-start(bf16[2,8,32,256]{3,2,1,0:T(8,128)(2,1)S(1)} %fusion.6) | copy-start | bytes 786436
  6.6 66.4 %copy-start.2 = (bf16[2,8,32,256]{3,2,1,0:T(8,128)(2,1)S(1)}, bf16[2,8,32,256]{3,2,1,0:T(8,128)(2,1)}, u32[]{:S(2)}) copy-start(bf16[2,8,32,256]{3,2,1,0:T(8,128)(2,1)} %param.5) | copy-start | bytes 786436
  6.6 66.4 %copy-start.3 = (bf16[2,8,32,256]{3,2,1,0:T(8,128)(2,1)S(1)}, bf16[2,8,32,256]{3,2,1,0:T(8,128)(2,1)}, u32[]{:S(2)}) copy-start(bf16[2,8,32,256]{3,2,1,0:T(8,128)(2,1)} %param.9) | copy-start | bytes 786436
  6.6 66.4 %copy-start.4 = (f32[256]{0:T(256)S(1)}, f32[256]{0:T(256)}, u32[]{:S(2)}) copy-start(f32[256]{0:T(256)} %param.6) | copy-start | bytes 3076
  73.0 2.4 %copy-start = (f32[1728,256]{1,0:T(8,128)S(1)}, f32[1728,256]{1,0:T(8,128)}, u32[]{:S(2)}) copy-start(f32[1728,256]{1,0:T(8,128)} %get-tuple-element.8) | copy-start | bytes 5308420

commit v2 on v1

--- a/solution.py
+++ b/solution.py
@@ -14,31 +14,18 @@
 TAPS = SIDE * SIDE
 
 
-def clip_tables(lengths, frame_ids):
-    order = jnp.arange(lengths.shape[0], dtype=jnp.int32)
-    clip_ends = jnp.sum(
-        jnp.where(order[None, :] <= order[:, None], lengths[None, :], 0), axis=1
-    ).astype(jnp.int32)
-    clip_starts = clip_ends - lengths
-    clip_ids = jnp.sum((frame_ids[:, None] >= clip_ends[None, :]).astype(jnp.int32), axis=1)
-    clip_first = jnp.max(
-        jnp.where(clip_starts[None, :] <= frame_ids[:, None], clip_starts[None, :], 0), axis=1
-    )
-    opening = jnp.any(clip_starts[None, :] == frame_ids[:, None], axis=1)
-    return (clip_ids, clip_first, opening)
-
-
 def kernel(
     dims,
-    table_ref,
-    coef_ref,
-    act_ref,
-    act_t_ref,
+    lengths_ref,
+    video_ref,
+    gain_ref,
     cot_ref,
     w_ref,
     out_ref,
     grad_ref,
     wgrad_ref,
+    table_ref,
+    act_t_ref,
     x_prev,
     x_own,
     cots,
@@ -52,6 +39,7 @@
     p_in,
     w_sem,
     xp_send,
+    xr_send,
     xp_recv,
     xo_send,
     xo_recv,
@@ -85,21 +73,51 @@
                     barrier, inc=1, device_id={"tm": tt, "chan": cc}, device_id_type=MESH
                 )
 
-    x_own[c] = act_ref[...]
+    gain = gain_ref[...]
+    for f in range(frames):
+        rows = slice(f * pixels, (f + 1) * pixels)
+        scaled = video_ref[rows, :].astype(jnp.float32) * gain
+        acted = (scaled / (1.0 + jnp.exp(-scaled))).astype(jnp.bfloat16)
+        x_own[c, rows, :] = acted
+        act_t_ref[:, rows] = acted.astype(jnp.float32).T.astype(jnp.bfloat16)
     cots[t] = cot_ref[...]
-    pl.semaphore_wait(barrier, n_tm * n_chan - 1)
+
+    starts, begun = [], jnp.int32(0)
+    for clip in range(lengths_ref.shape[0]):
+        starts.append(begun)
+        begun = begun + lengths_ref[clip]
+
+    def first_of(frame):
+        value = jnp.int32(0)
+        for begun_at in starts[1:]:
+            value = jnp.where(begun_at <= frame, begun_at, value)
+        return jnp.where(frame >= begun, begun, value)
+
+    def note(frame, _):
+        first = first_of(frame)
+        for lag in range(LAGS):
+            table_ref[frame * LAGS + lag] = jnp.maximum(frame - lag, first)
+        return 0
+
+    lax.fori_loop(0, n_tm * frames, note, 0)
 
     def send_own(cc):
         return pltpu.make_async_remote_copy(
-            act_ref, x_own.at[c], xo_send.at[cc], xo_recv.at[c],
+            x_own.at[c], x_own.at[c], xo_send.at[cc], xo_recv.at[c],
             device_id={"chan": cc}, device_id_type=MESH,
         )
 
-    def send_prev(cc):
+    def send_prev():
         return pltpu.make_async_remote_copy(
-            act_ref.at[pl.ds((frames - 2) * pixels, 2 * pixels)], x_prev.at[c],
-            xp_send.at[cc], xp_recv.at[c],
-            device_id={"tm": t + 1, "chan": cc}, device_id_type=MESH,
+            x_own.at[c, pl.ds((frames - 2) * pixels, 2 * pixels)], x_prev.at[c],
+            xp_send.at[c], xp_recv.at[c],
+            device_id={"tm": t + 1}, device_id_type=MESH,
+        )
+
+    def pass_prev(cc):
+        return pltpu.make_async_remote_copy(
+            x_prev.at[c], x_prev.at[c], xr_send.at[cc], xp_recv.at[c],
+            device_id={"chan": cc}, device_id_type=MESH,
         )
 
     def send_cot(s, way, to):
@@ -109,9 +127,7 @@
         )
 
     def send_at(tt, cc):
-        row = (tt * n_rows + r) * block - c * own
-        if n_rows > 1:
-            row = pl.multiple_of(row, 16)
+        row = pl.multiple_of((tt * n_rows + r) * block - c * own, 16)
         return pltpu.make_async_remote_copy(
             act_t_ref.at[pl.ds(row, block)], act_ts.at[t], at_send.at[tt, cc], at_recv.at[t],
             device_id={"tm": tt, "chan": cc}, device_id_type=MESH,
@@ -167,21 +183,10 @@
             arrived(cots.at[s], cot_recv.at[s])
             cot_moves(s, False, start_cot)
 
-    cot_moves(t, None, start_cot)
-    for cc in range(n_chan):
-
-        @pl.when(cc != c)
-        def _():
-            send_own(cc).start()
-
-        @pl.when(t + 1 < n_tm)
-        def _():
-            send_prev(cc).start()
-
-    for_at(lambda tt, cc: send_at(tt, cc).start())
     row0 = (t * n_rows + r) * block
-
-    @pl.when(row0 // own == c)
+    for_owner = row0 // own != c
+
+    @pl.when(jnp.logical_not(for_owner))
     def _():
         act_ts[t] = act_t_ref[pl.ds(pl.multiple_of(row0 - c * own, 16), block), :]
 
@@ -203,47 +208,76 @@
     pad_x[:, :, edge:, :] = jnp.zeros_like(pad_x[:, :, edge:, :])
     pad_g[:, :, :, :width, :] = jnp.zeros_like(pad_g[:, :, :, :width, :])
     pad_g[:, :, :, edge:, :] = jnp.zeros_like(pad_g[:, :, :, edge:, :])
-    partial[...] = jnp.zeros_like(partial)
-    out_ref[...] = jnp.zeros_like(out_ref)
-    wgrad_ref[...] = jnp.zeros_like(wgrad_ref)
-
-    if places > 1:
-        hop(1)
-
-    if pair == 2:
-
-        @pl.when(side == 0)
-        def _():
-            arrived(cots.at[sibling], cot_recv.at[sibling])
-
-        @pl.when((side == 1) & (t + 1 < n_tm))
-        def _():
-            arrived(cots.at[t + 1], cot_recv.at[t + 1])
+
+    def fill_own(cc):
+        for f in range(frames):
+            value = x_own[cc, f * pixels : (f + 1) * pixels, :].astype(jnp.float32)
+            lanes = pl.ds(pl.multiple_of(cc * own, 128), own)
+            fill(pad_x.at[2 + f, :, :, lanes], value, 1)
 
     def cot_frame(f):
         frame = jnp.minimum(t * frames + f, n_tm * frames - 1)
-        return cots[frame // frames, pl.ds((frame % frames) * pixels, pixels), :].astype(jnp.float32)
+        rows = pl.ds(pl.multiple_of((frame % frames) * pixels, 16), pixels)
+        return cots[frame // frames, rows, :].astype(jnp.float32)
 
     for f in range(frames):
-        near = [cot_frame(f + m) for m in range(LAGS)]
-        for lag in range(LAGS):
-            mixed = sum(coef_ref[(f * LAGS + lag) * LAGS + m] * near[m] for m in range(lag + 1))
-            fill(pad_g.at[f, lag], mixed, -1)
+        fill(pad_g.at[f, 0], cot_ref[f * pixels : (f + 1) * pixels, :].astype(jnp.float32), -1)
+    fill_own(c)
+
+    pl.semaphore_wait(barrier, n_tm * n_chan - 1)
+    cot_moves(t, None, start_cot)
+    for cc in range(n_chan):
+
+        @pl.when(cc != c)
+        def _():
+            send_own(cc).start()
+
+    @pl.when(t + 1 < n_tm)
+    def _():
+        send_prev().start()
 
     load_w.wait()
 
-    def back(k, _):
-        lag, a, b = k // TAPS, (k % TAPS) // SIDE, k % SIDE
-        start = pl.multiple_of((r * height + 2 - a) * width, 16)
-        grads = jnp.concatenate(
-            [pad_g[f, lag, b, pl.ds(start, local), :] for f in range(frames)], axis=0
-        )
-        partial[...] += lax.dot_general(
-            grads, w_buf[k], (((1,), (1,)), ((), ())), preferred_element_type=jnp.float32
-        )
-        return 0
-
-    lax.fori_loop(0, LAGS * TAPS, back, 0)
+    def back(lag):
+        for a in range(SIDE):
+            start = pl.multiple_of((r * height + 2 - a) * width, 16)
+            grads = jnp.concatenate(
+                [
+                    jnp.concatenate(
+                        [pad_g[f, lag, b, pl.ds(start, local), :] for b in range(SIDE)], axis=1
+                    )
+                    for f in range(frames)
+                ],
+                axis=0,
+            )
+            k = lag * TAPS + a * SIDE
+            kernels = jnp.concatenate([w_buf[k + b] for b in range(SIDE)], axis=1)
+            found = lax.dot_general(
+                grads, kernels, (((1,), (1,)), ((), ())), preferred_element_type=jnp.float32
+            )
+            if lag == 0 and a == 0:
+                partial[...] = found
+            else:
+                partial[...] += found
+
+    def ahead(lag):
+        for a in range(SIDE):
+            start = pl.multiple_of((r * height + a) * width, 16)
+
+            def taps_of(f):
+                slot = table_ref[t * frames * LAGS + f * LAGS + lag] - t * frames + 2
+                return jnp.concatenate(
+                    [pad_x[slot, b, pl.ds(start, local), :] for b in range(SIDE)], axis=1
+                )
+
+            taps = jnp.concatenate([taps_of(f) for f in range(frames)], axis=0)
+            k = lag * TAPS + a * SIDE
+            kernels = w_buf[k : k + SIDE].reshape(-1, own)
+            found = jnp.dot(taps, kernels, preferred_element_type=jnp.float32)
+            if lag == 0 and a == 0:
+                out_ref[...] = found
+            else:
+                out_ref[...] += found
 
     def send_p(cc):
         return pltpu.make_async_remote_copy(
@@ -251,6 +285,59 @@
             device_id={"chan": cc}, device_id_type=MESH,
         )
 
+    hops = iter(range(1, places))
+
+    def advance():
+        for d in hops:
+            hop(d)
+            break
+
+    back(0)
+    advance()
+    for_at(lambda tt, cc: send_at(tt, cc).start())
+    for cc in range(n_chan):
+
+        @pl.when(cc != c)
+        def _():
+            arrived(x_own.at[cc], xo_recv.at[cc])
+            fill_own(cc)
+
+    ahead(0)
+    advance()
+
+    @pl.when(t > 0)
+    def _():
+        arrived(x_prev.at[c], xp_recv.at[c])
+        for cc in range(n_chan):
+
+            @pl.when(cc != c)
+            def _():
+                pass_prev(cc).start()
+
+    if pair == 2:
+
+        @pl.when(side == 0)
+        def _():
+            arrived(cots.at[sibling], cot_recv.at[sibling])
+
+        @pl.when((side == 1) & (t + 1 < n_tm))
+        def _():
+            arrived(cots.at[t + 1], cot_recv.at[t + 1])
+
+    for f in range(frames):
+        here = t * frames + f
+        opens = first_of(here) == here
+        near = [cot_frame(f + m) for m in range(LAGS)]
+        same = [(first_of(here + m) == first_of(here)) & (here + m < begun) for m in range(LAGS)]
+        for lag in range(1, LAGS):
+            mixed = jnp.where(same[lag], near[lag], 0.0)
+            for m in range(lag):
+                mixed = mixed + jnp.where(same[m] & opens, near[m], 0.0)
+            fill(pad_g.at[f, lag], mixed, -1)
+
+    back(1)
+    advance()
+    back(2)
     for cc in range(n_chan):
 
         @pl.when(cc != c)
@@ -258,54 +345,25 @@
             p_out[cc] = partial[:, cc * own : (cc + 1) * own].astype(jnp.bfloat16)
             send_p(cc).start()
 
-    if places > 2:
-        hop(2)
-
+    advance()
     for cc in range(n_chan):
 
-        @pl.when(cc != c)
-        def _():
-            arrived(x_own.at[cc], xo_recv.at[cc])
-
-        @pl.when(t > 0)
+        @pl.when((t > 0) & (cc != c))
         def _():
             arrived(x_prev.at[cc], xp_recv.at[cc])
 
-    for cc in range(n_chan):
-        for slot in range(2 + frames):
-            if slot < 2:
-                value = x_prev[cc, slot * pixels : (slot + 1) * pixels, :]
-            else:
-                value = x_own[cc, (slot - 2) * pixels : (slot - 1) * pixels, :]
-            fill(
-                pad_x.at[slot, :, :, cc * own : (cc + 1) * own], value.astype(jnp.float32), 1
-            )
-
-    if places > 3:
-        hop(3)
-
-    def ahead(k, _):
-        lag, a, b = k // TAPS, (k % TAPS) // SIDE, k % SIDE
-        start = pl.multiple_of((r * height + a) * width, 16)
-        taps = jnp.concatenate(
-            [
-                pad_x[table_ref[f * LAGS + lag], b, pl.ds(start, local), :]
-                for f in range(frames)
-            ],
-            axis=0,
-        )
-        out_ref[...] += jnp.dot(taps, w_buf[k], preferred_element_type=jnp.float32)
-        return 0
-
-    lax.fori_loop(0, LAGS * TAPS, ahead, 0)
-
-    for d in range(4, places):
+        for slot in range(2):
+            value = x_prev[cc, slot * pixels : (slot + 1) * pixels, :].astype(jnp.float32)
+            fill(pad_x.at[slot, :, :, cc * own : (cc + 1) * own], value, 1)
+
+    ahead(1)
+    advance()
+    ahead(2)
+    for d in hops:
         hop(d)
 
     place_of = lax.broadcasted_iota(jnp.int32, (1, pixels), 1)
     line, spot = place_of // width, place_of % width
-
-    for_owner = row0 // own != c
 
     def build(s, _):
         @pl.when((s != t) | for_owner)
@@ -344,7 +402,7 @@
         for lag in range(LAGS):
             taps = jnp.concatenate(
                 [
-                    stack[table_ref[frames * LAGS + (s * frames + f) * LAGS + lag]]
+                    stack[table_ref[(s * frames + f) * LAGS + lag]]
                     for f in range(frames)
                 ],
                 axis=1,
@@ -353,6 +411,7 @@
             wgrad_ref[rows, :] += jnp.dot(taps, cots[s], preferred_element_type=jnp.float32)
         return 0
 
+    wgrad_ref[...] = jnp.zeros_like(wgrad_ref)
     lax.fori_loop(0, n_tm, weigh, 0)
 
     total = partial[:, pl.ds(pl.multiple_of(c * own, 128), own)]
@@ -366,9 +425,13 @@
             send_p(cc).wait_send()
             send_own(cc).wait_send()
 
-        @pl.when(t + 1 < n_tm)
-        def _():
-            send_prev(cc).wait_send()
+        @pl.when((t > 0) & (cc != c))
+        def _():
+            pass_prev(cc).wait_send()
+
+    @pl.when(t + 1 < n_tm)
+    def _():
+        send_prev().wait_send()
 
     for_at(lambda tt, cc: send_at(tt, cc).wait_send())
     cot_moves(t, None, finish_cot)
@@ -391,33 +454,15 @@
     total_pixels = local_count * n_tm * n_rows
     all_frames = n_tm * frame_count
     block = all_chans // (n_tm * n_rows)
-    frame_base = lax.axis_index("tm") * frame_count
-    frame_ids = jnp.arange(all_frames + 2, dtype=jnp.int32)
-    clip_ids, clip_first, opening = clip_tables(lengths, frame_ids)
-    lags = jnp.arange(LAGS, dtype=jnp.int32)
-    sources = jnp.maximum(frame_ids[:all_frames, None] - lags, clip_first[:all_frames, None])
-    mine = lax.dynamic_slice_in_dim(sources, frame_base, frame_count, 0)
-    table = jnp.concatenate([(mine - frame_base + 2).reshape(-1), sources.reshape(-1)])
-    ids = lax.dynamic_slice_in_dim(clip_ids, frame_base, frame_count + 2, 0)
-    opens = lax.dynamic_slice_in_dim(opening, frame_base, frame_count, 0)
-    same = jnp.stack([ids[m : m + frame_count] == ids[:frame_count] for m in range(LAGS)], axis=1)
-    coef = jnp.where(
-        lags[None, :, None] == lags[None, None, :],
-        same[:, None, :],
-        (lags[None, None, :] < lags[None, :, None]) & same[:, None, :] & opens[:, None, None],
-    ).astype(jnp.float32).reshape(-1)
-
     scaled = video.astype(jnp.float32) * channel_gain
-    activated = jax.nn.silu(scaled).astype(jnp.bfloat16)
-    act_full, cot_full = activated, cotangent
+    video_full, cot_full = video, cotangent
     if n_rows > 1:
-        act_full = lax.all_gather(activated, "rows", axis=1, tiled=True)
+        video_full = lax.all_gather(video, "rows", axis=1, tiled=True)
         cot_full = lax.all_gather(cotangent, "rows", axis=1, tiled=True)
-    act_full = act_full.reshape(-1, own)
+    video_full = video_full.reshape(-1, own)
     cot_full = cot_full.reshape(-1, own)
-    act_t = act_full.T
-
-    full = act_full.shape[0]
+
+    full = video_full.shape[0]
     pixels = full // frame_count
     padded = pixels + 2 * col_count
     vmem = pl.BlockSpec(memory_space=pltpu.VMEM)
@@ -433,9 +478,11 @@
             jax.ShapeDtypeStruct((local_count, own), f32),
             jax.ShapeDtypeStruct((taps * block, own), f32),
         ),
-        in_specs=[smem, smem, vmem, vmem, vmem, pl.BlockSpec(memory_space=pl.ANY)],
+        in_specs=[smem, vmem, vmem, vmem, pl.BlockSpec(memory_space=pl.ANY)],
         out_specs=(vmem, vmem, vmem),
         scratch_shapes=[
+            pltpu.SMEM((all_frames * LAGS,), jnp.int32),
+            pltpu.VMEM((own, full), bf16),
             pltpu.VMEM((n_chan, 2 * pixels, own), bf16),
             pltpu.VMEM((n_chan, full, own), bf16),
             pltpu.VMEM((n_tm, full, own), bf16),
@@ -452,6 +499,7 @@
             dma((n_chan,)),
             dma((n_chan,)),
             dma((n_chan,)),
+            dma((n_chan,)),
             dma((3, n_tm)),
             dma((n_tm,)),
             dma((n_tm, n_chan)),
@@ -467,7 +515,7 @@
             bytes_accessed=2 * weights.size + 4 * taps * block * own,
             transcendentals=0,
         ),
-    )(table, coef, act_full, act_t, cot_full, weights)
+    )(lengths, video_full, channel_gain.reshape(1, own), cot_full, weights)
 
     output = (video.astype(f32) + out_sum.reshape(video.shape)).astype(bf16)
     sigmoid_value = jax.nn.sigmoid(scaled)

time: 77.2 us -> 65 us (0.84)
  Pallas kernels: 66.4 us -> 60.4 us
  other arithmetic: 7.9 us -> 3.71 us
  local copies, waits for them, and re-layouts: 1.75 us -> 0.02 us
    pallas_call x1, Pallas kernels: 66.4 us -> 60.4 us  [shards(): pl.pallas_call(functools.partial(kernel, (n_tm, n_chan, n_rows, frame_cou...]
    convert_element_type x2 -> x0, other arithmetic: 1.67 us -> none  [the longest x1 1.1 us: shards(): activated = jax.nn.silu(scaled).astype(jnp.bfloat16)]
    reshape x2 -> x0, local copies, waits for them, and re-layouts: 0.93 us -> none  [the longest x1 0.84 us: shards(): act_full = act_full.reshape(-1, own)]
    reduce_sum x2 -> x0, other arithmetic: 0.86 us -> none  [the longest x1 0.77 us: clip_tables(): jnp.sum(jnp.where(order[None, :] <= order[:, None], lengths[None, :], 0),...]
where the time goes in v2:
time: 65 us; the launch traced here: 64.8 us
  Pallas kernels  60.4 us (93%)
  other arithmetic  3.71 us (6%)
  between operations  0.7 us (1%)
    pallas_call x1, Pallas kernels, shards(): pl.pallas_call(functools.partial(kernel, (n_tm, n_chan, n_rows, frame_cou...  60.4 us
    convert_element_type x1, other arithmetic, shards(): input_grad = (cotangent.astype(f32) + act_grad.reshape(video.shape) * slo...  2.39 us
    mul x1, other arithmetic, shards(): weight_sum.reshape(taps, block, own) * (1.0 / math.sqrt(total_pixels))  1.32 us

profile of v2, /device:TPU:0, one launch (start us, length us, event | category | flops | bytes accessed | tf_op | source)
XLA Modules:
  0.0 64.8 jit_solution(4554574489019668035)
XLA Ops:
  0.6 0.0 copy-start.1
  0.6 0.0 copy-start.2
  0.7 0.0 copy-start.3
  0.7 60.4 %shard_map.76 = (f32[512,256]{1,0:T(8,128)}, f32[512,256]{1,0:T(8,128)}, f32[1728,256]{1,0:T(8,128)}) custom-call(s32[4]{0:T(128)} %lengths_ref.1, bf16[512,256]{1,0:T(8,128)(2,1)} %bitcast.9, f32[1,256]{1,0:T(1,128)} %bitcast.11, bf16[512,256]{1,0:T(8,128)(2,1)} %bitcast.10, bf16[27,512,256]{2,1,0:T(8,128)(2,1)} %w_ref.1), custom_call_target="tpu_custom_call" | custom-call | flops 10871635968 | bytes 8847360 | tf_op jit(solution)/shard_map/pallas_call | solution.py:472
  61.1 0.0 copy-start
  61.1 0.0 copy-done.1
  61.1 0.0 copy-done.2
  61.1 0.0 copy-done.3
  61.1 2.4 %fusion.10 = (bf16[2,8,32,256]{3,2,1,0:T(8,128)(2,1)}, bf16[2,8,32,256]{3,2,1,0:T(8,128)(2,1)}) fusion(f32[2,8,32,256]{3,2,1,0:T(8,128)} %bitcast.8, bf16[2,8,32,256]{3,2,1,0:T(8,128)(2,1)S(1)} %copy-done.1, bf16[2,8,32,256]{3,2,1,0:T(8,128)(2,1)S(1)} %copy-done.2, f32[256]{0:T(256)S(1)} %copy-done.3, f32[2,8,32,256]{3,2,1,0:T(8,128)} %bitcast.7), kind=kLoop, calls=%fused_computation.13 | loop fusion | flops 2097152 | bytes 2098176 | tf_op jit(solution)/shard_map/convert_element_type | solution.py:525
  63.5 0.0 copy-done
  63.5 1.3 %broadcast_multiply_fusion = f32[1728,256]{1,0:T(8,128)} fusion(f32[1728,256]{1,0:T(8,128)S(1)} %copy-done), kind=kLoop, calls=%fused_computation | loop fusion | flops 442368 | bytes 3538944 | tf_op jit(solution)/shard_map/mul | solution.py:526
Async XLA Ops:
  0.6 60.4 %copy-start.1 = (bf16[2,8,32,256]{3,2,1,0:T(8,128)(2,1)S(1)}, bf16[2,8,32,256]{3,2,1,0:T(8,128)(2,1)}, u32[]{:S(2)}) copy-start(bf16[2,8,32,256]{3,2,1,0:T(8,128)(2,1)} %param.5) | copy-start | bytes 786436
  0.6 60.4 %copy-start.2 = (bf16[2,8,32,256]{3,2,1,0:T(8,128)(2,1)S(1)}, bf16[2,8,32,256]{3,2,1,0:T(8,128)(2,1)}, u32[]{:S(2)}) copy-start(bf16[2,8,32,256]{3,2,1,0:T(8,128)(2,1)} %param.9) | copy-start | bytes 786436
  0.7 60.4 %copy-start.3 = (f32[256]{0:T(256)S(1)}, f32[256]{0:T(256)}, u32[]{:S(2)}) copy-start(f32[256]{0:T(256)} %param.6) | copy-start | bytes 3076
  61.1 2.4 %copy-start = (f32[1728,256]{1,0:T(8,128)S(1)}, f32[1728,256]{1,0:T(8,128)}, u32[]{:S(2)}) copy-start(f32[1728,256]{1,0:T(8,128)} %get-tuple-element.8) | copy-start | bytes 5308420
